TPU v7x, 128 devices: a whole 4x4x4 slice. The times are simulated.
128 devices in a mesh: passage: 32 (over x, z_hi, y), span: 4 (over z_lo, core).
Axes of the slice: x: 4, y: 4, z: 4 (z_hi: 2, z_lo: 2; z = z_hi * 2 + z_lo), core: 2. Of those that a mesh axis runs over, the one named last changes fastest.
Arguments:
- adjoint: float32 [5, 32, 128, 1024], P(None, 'span', 'passage'), may hold values from -6 to 6
- forcing: float32 [5, 32, 128, 1024], P(None, 'span', 'passage'), may hold values from -6 to 6
- area_scale: float32 [1, 32, 128, 1024], P(None, 'span', 'passage'), may hold values from 0.5 to 2
- azimuth_coupling: float32 [5, 5], replicated, may hold values from -2 to 2
- axial_coupling: float32 [5, 5], replicated, may hold values from -2 to 2
- inverse: float32 [8, 160, 160], P('span'), as said below
- owner_device: int32 [4, 128, 8, 1], P('span', 'passage'), may hold values from 0 to 31; in each aligned block of 32 rows (0 to 31, 32 to 63, ..., all dimensions but the last counted through in order) at most 2 rows name the same one
- owner_slot: int32 [4, 128, 8, 1], P('span', 'passage'), may hold values from 0 to 3
- weight: float32 [4, 128, 8, 1], P('span', 'passage'), may hold values from 0.5 to 1.5
Outputs:
- adjoint_out: float32 [5, 32, 128, 1024], P(None, 'span', 'passage')
Inputs may be any that keep to these rules, and one draw needn't show every extreme that they name: `owner_device`: within the inlet points of one device (aligned blocks of 32 entries in order), at most 2 name one passage index; some block reaches 2. Each block is the inverse of a nonsingular radial operator; entries are of order one on the diagonal.
All inputs are finite; a program needn't handle non-finite values.
Results may differ from a plain program's by a relative error of at most 0.00012.
Values sent between devices are 32-bit elements; how exact they have to be, the bound alone decides.
A program may use at most 64 MiB of HBM per device.

v0:
```python
import jax
import jax.numpy as jnp
from jax import lax
from jax.experimental import pallas as pl
from jax.experimental.pallas import tpu as pltpu
from jax.sharding import PartitionSpec as P

ITERS = 4
MESH = pl.DeviceIdType.MESH
NF = 5
R = 8
NR = 32
ROWS = NF * NR
A = 4
CH = 32
TILES = 8
PLANES = 4
FOLD = 40
F32 = jnp.float32
BF16 = jnp.bfloat16


def lanes(shape):
    return lax.broadcasted_iota(jnp.int32, shape, len(shape) - 1)


def roll(x, by):
    by = by % 128
    return x if by == 0 else pltpu.roll(x, by, x.ndim - 1)


def swap_groups(v, lane):
    half = lane < 64
    odd = (lane // 32) % 2 == 1
    c0 = jnp.where(half, v[0], roll(v[2], 64))
    c2 = jnp.where(half, roll(v[0], 64), v[2])
    c1 = jnp.where(half, v[1], roll(v[3], 64))
    c3 = jnp.where(half, roll(v[1], 64), v[3])
    return [
        jnp.where(odd, roll(c1, 32), c0),
        jnp.where(odd, c1, roll(c0, 96)),
        jnp.where(odd, roll(c3, 32), c2),
        jnp.where(odd, c3, roll(c2, 96)),
    ]


def split(x):
    high = x.astype(BF16)
    return high, (x - high.astype(F32)).astype(BF16)


def kernel(
    adj, frc, area, azc, axc, inv, tsend, out,
    sbuf, ext, fa, psend, hal, inl, obuf, tab, tpl, tall, mtab, lhs, rhs, exitb,
    a_send, a_recv, f_send, f_recv, o_send, o_recv,
    az_send, az_recv, ax_send, ax_recv, ex_send, ex_recv,
    t_send, t_recv, u_send, u_recv,
):
    p = lax.axis_index("passage")
    s = lax.axis_index("span")
    plane = p // TILES
    k = p % TILES
    c = s * TILES + k
    first = c == 0
    last = c == CH - 1

    def device(plane_at, chunk):
        return (plane_at * TILES + chunk % TILES, chunk // TILES)

    def remote(src, dst, send, recv, to):
        return pltpu.make_async_remote_copy(
            src_ref=src, dst_ref=dst, send_sem=send, recv_sem=recv,
            device_id=to, device_id_type=MESH,
        )

    def own_rows(span):
        return pl.ds(pl.multiple_of(span * R, R), R)

    barrier = pltpu.get_barrier_semaphore()

    def greet(plane_at, chunk):
        pl.semaphore_signal(barrier, inc=1, device_id=device(plane_at, chunk), device_id_type=MESH)

    def greet_group(t, carry):
        greet(plane, (c + t) % CH)
        return carry

    lax.fori_loop(1, CH, greet_group, 0)
    for d in range(1, PLANES):
        greet((plane + d) % PLANES, c)

    @pl.when(first)
    def _():
        for d in range(1, PLANES):
            greet((plane + d) % PLANES, CH - 1)

    @pl.when(last)
    def _():
        for d in range(1, PLANES):
            greet((plane + d) % PLANES, 0)

    lane8 = lanes((R, 128))

    def regroup(src, field, slot):
        def body(t, carry):
            at = pl.ds(pl.multiple_of(t * 128, 128), 128)
            pieces = swap_groups([src[field, :, j, at] for j in range(A)], lane8)
            for i in range(A):
                sbuf[t * A + i, slot] = pieces[i]
            return carry

        lax.fori_loop(0, CH // A, body, 0)

    for f in range(NF):
        regroup(adj, f, f)
    hal[...] = jnp.zeros_like(hal)

    edge = jnp.logical_or(first, last)
    peers = CH - 1 + PLANES - 1

    @pl.when(edge)
    def _():
        pl.semaphore_wait(barrier, peers + PLANES - 1)

    @pl.when(jnp.logical_not(edge))
    def _():
        pl.semaphore_wait(barrier, peers)

    def adj_copy(to, source):
        return remote(
            sbuf.at[to, pl.ds(0, NF)],
            ext.at[0, 1 + source % TILES, :, own_rows(source // TILES), :],
            a_send.at[to], a_recv.at[source], device(plane, to),
        )

    def frc_copy(to, source):
        return remote(
            sbuf.at[to, pl.ds(NF, NF + 1)],
            fa.at[source % TILES, :, own_rows(source // TILES), :],
            f_send.at[to], f_recv.at[source], device(plane, to),
        )

    def out_copy(to, source):
        return remote(
            ext.at[ITERS, 1 + to % TILES, :, own_rows(to // TILES), :],
            obuf.at[source],
            o_send.at[to], o_recv.at[source], device(plane, to),
        )

    def over_group(do):
        def body(t, carry):
            do((c + t) % CH)
            return carry

        lax.fori_loop(1, CH, body, 0)

    over_group(lambda to: adj_copy(to, c).start())

    table_copy = remote(
        tsend, tab.at[k, own_rows(s), :], t_send, t_recv.at[c], device(plane, CH - 1)
    )

    @pl.when(jnp.logical_not(last))
    def _():
        table_copy.start()

    for f in range(NF):
        regroup(frc, f, NF + f)
    regroup(area, 0, 2 * NF)
    over_group(lambda to: frc_copy(to, c).start())

    ext[0, 1 + k, :, own_rows(s), :] = sbuf[c, 0:NF]
    fa[k, :, own_rows(s), :] = sbuf[c, NF:2 * NF + 1]

    high, low = split(inv[k // (TILES // 2)])
    lhs[0] = high
    lhs[1] = low

    xx32 = lanes((NR, 128)) % 32
    lane160 = lanes((ROWS, 128))
    xx160 = lane160 % 32
    lane40 = lanes((FOLD, 128))
    xx40 = lane40 % 32

    def plane_table(plane_to):
        return remote(
            tpl, tall.at[plane], u_send.at[plane_to], u_recv.at[plane],
            device(plane_to, CH - 1),
        )

    def plane_table_in(plane_from):
        return remote(
            tpl, tall.at[plane_from], u_send.at[plane_from], u_recv.at[plane_from],
            device(plane_from, CH - 1),
        )

    @pl.when(last)
    def _():
        tab[k, own_rows(s), :] = tsend[...]

        def arrived(source, carry):
            remote(
                tsend, tab.at[source % TILES, own_rows(source // TILES), :],
                t_send, t_recv.at[source], device(plane, 0),
            ).wait_recv()
            return carry

        lax.fori_loop(0, CH - 1, arrived, 0)
        merged = jnp.zeros((NR, 128), F32)
        for i in range(TILES):
            merged = jnp.where((xx32 == i) | (xx32 == 16 + i), tab[i], merged)
        tpl[...] = merged
        for d in range(1, PLANES):
            plane_table((plane + d) % PLANES).start()
        tall[plane] = merged
        for d in range(1, PLANES):
            plane_table_in((plane + d) % PLANES).wait_recv()
        column = jnp.zeros((NR, 128), F32)
        weight = jnp.zeros((NR, 128), F32)
        for i in range(PLANES):
            mine = xx32 // 8 == i
            column = jnp.where(mine, roll(tall[i], 8 * i), column)
            weight = jnp.where(mine, roll(tall[i], 8 * i - 16), weight)
        column = column.astype(jnp.int32) - plane * 32

        def masked(b, carry):
            mtab[b] = jnp.where(column == b, weight, 0.0)
            return carry

        lax.fori_loop(0, 32, masked, 0)
        for d in range(1, PLANES):
            plane_table((plane + d) % PLANES).wait_send()

    up = (plane + 1) % PLANES
    down = (plane + PLANES - 1) % PLANES
    nxt = (c + 1) % CH
    prv = (c + CH - 1) % CH

    def az_copy(n, side):
        if side == 0:
            return remote(ext.at[n, 1], ext.at[n, TILES + 1], az_send.at[n, 0], az_recv.at[n, 0], device(down, c))
        return remote(ext.at[n, TILES], ext.at[n, 0], az_send.at[n, 1], az_recv.at[n, 1], device(up, c))

    def ax_copy(n, side):
        if side == 0:
            return remote(psend.at[n, 0], hal.at[n, 1], ax_send.at[n, 0], ax_recv.at[n, 1], device(plane, prv))
        return remote(psend.at[n, 1], hal.at[n, 0], ax_send.at[n, 1], ax_recv.at[n, 0], device(plane, nxt))

    def ax_wait(n, side):
        return remote(psend.at[n, side], hal.at[n, side], ax_send.at[n, side], ax_recv.at[n, side], device(plane, nxt))

    def ex_copy(n, to):
        return remote(psend.at[n, 0], inl.at[n, plane], ex_send.at[n, to], ex_recv.at[n, plane], device(to, CH - 1))

    def ex_wait(n, source):
        return remote(psend.at[n, 0], inl.at[n, source], ex_send.at[n, source], ex_recv.at[n, source], device(source, 0))

    def send_az(n):
        for side in range(2):
            az_copy(n, side).start()

    def send_ax(n):
        edges = [jnp.zeros((FOLD, 128), F32), jnp.zeros((FOLD, 128), F32)]
        for kk in range(TILES):
            tile = ext[n, 1 + kk].reshape(ROWS, 128)
            for g in range(4):
                rows = tile[g * FOLD:(g + 1) * FOLD]
                to = 8 * g + kk
                edges[0] = jnp.where(xx40 == to, roll(rows, to), edges[0])
                edges[1] = jnp.where(xx40 == to, roll(rows, to - 31), edges[1])
        psend[n, 0] = edges[0]
        psend[n, 1] = edges[1]

        @pl.when(jnp.logical_not(first))
        def _():
            ax_copy(n, 0).start()

        @pl.when(jnp.logical_not(last))
        def _():
            ax_copy(n, 1).start()

        @pl.when(first)
        def _():
            for to in range(PLANES):
                ex_copy(n, to).start()

    def wait_adj(source):
        adj_copy(source, source).wait_recv()

    def wait_frc(source):
        frc_copy(source, source).wait_recv()

    over_group(wait_adj)
    send_az(0)
    send_ax(0)
    over_group(wait_frc)

    az = [[azc[f, g] * (1.0 / 12.0) for g in range(NF)] for f in range(NF)]
    ax = [[axc[f, g] * 0.5 for g in range(NF)] for f in range(NF)]

    def couple(coefficients, slope, f):
        total = coefficients[f][0] * slope[0:NR]
        for g in range(1, NF):
            total = total + coefficients[f][g] * slope[g * NR:(g + 1) * NR]
        return total

    def azimuth_part(n, kk):
        here = ext[n, 1 + kk].reshape(ROWS, 128)
        before = ext[n, kk].reshape(ROWS, 128)
        after = ext[n, 2 + kk].reshape(ROWS, 128)
        plus = roll(jnp.where(lane160 >= 32, here, after), 96)
        minus = roll(jnp.where(lane160 < 96, here, before), 32)
        far = roll(
            jnp.where(lane160 >= 64, here, after) - jnp.where(lane160 < 64, here, before), 64
        )
        slope = 8.0 * (plus - minus) - far
        at = slice(kk * 128, (kk + 1) * 128)
        for f in range(NF):
            rows = slice(f * NR, (f + 1) * NR)
            rhs[rows, at] = here[rows] + fa[kk, f] - fa[kk, NF] * couple(az, slope, f)

    def axial_part(n, kk, before, after):
        here = ext[n, 1 + kk].reshape(ROWS, 128)
        slope = jnp.where(xx160 == 31, roll(after, 31 - kk), roll(here, 127)) - jnp.where(
            xx160 == 0, roll(before, -kk), roll(here, 1)
        )
        at = slice(kk * 128, (kk + 1) * 128)
        for f in range(NF):
            rows = slice(f * NR, (f + 1) * NR)
            rhs[rows, at] = rhs[rows, at] - fa[kk, NF] * couple(ax, slope, f)

    def unfold(edge):
        return jnp.concatenate([roll(edge, -8 * g) for g in range(4)], axis=0)

    def exit_plane(n):
        for source in range(PLANES):
            ex_wait(n, source).wait_recv()
        groups = []
        for g in range(4):
            group = jnp.zeros((FOLD, 128), F32)
            for i in range(PLANES):
                group = jnp.where(xx40 // 8 == i, roll(inl[n, i], 8 * (i - g)), group)
            groups.append(group)
        inlet = jnp.concatenate(groups, axis=0)
        exitb[...] = jnp.zeros_like(exitb)
        column = lanes((256, 128))

        def one(b, carry):
            weighted = inlet * jnp.concatenate([mtab[b]] * NF, axis=0)
            pair = jnp.concatenate(split(weighted), axis=1)
            place = (b % A) * 32 + b // A
            ones = (column == place).astype(F32).astype(BF16)
            exitb[...] += jnp.dot(pair, ones, preferred_element_type=F32)
            return carry

        lax.fori_loop(0, 32, one, 0)
        arrived = exitb[...]
        for kk in range(TILES):
            at = slice(kk * 128, (kk + 1) * 128)
            rhs[:, at] = rhs[:, at] + jnp.where(xx160 == 31, roll(arrived, 31 - kk), 0.0)

    def solve(n, pair):
        high, low = split(rhs[:, pair * 256:(pair + 1) * 256])
        solved = jnp.dot(lhs[0], low, preferred_element_type=F32)
        solved = solved + jnp.dot(lhs[1], high, preferred_element_type=F32)
        solved = solved + jnp.dot(lhs[0], high, preferred_element_type=F32)
        for i in range(2):
            ext[n + 1, 1 + 2 * pair + i] = solved[:, i * 128:(i + 1) * 128].reshape(NF, NR, 128)

    def sweep(n, carry):
        for kk in range(1, TILES - 1):
            azimuth_part(n, kk)
        for side in range(2):
            az_copy(n, side).wait_recv()
        azimuth_part(n, 0)
        azimuth_part(n, TILES - 1)

        @pl.when(jnp.logical_not(first))
        def _():
            ax_wait(n, 0).wait_recv()

        @pl.when(jnp.logical_not(last))
        def _():
            ax_wait(n, 1).wait_recv()

        before = unfold(hal[n, 0])
        after = unfold(hal[n, 1])
        for kk in range(TILES):
            axial_part(n, kk, before, after)

        @pl.when(last)
        def _():
            exit_plane(n)

        solve(n, 0)
        solve(n, 3)

        @pl.when(n < ITERS - 1)
        def _():
            send_az(n + 1)

        solve(n, 1)
        solve(n, 2)

        @pl.when(n < ITERS - 1)
        def _():
            send_ax(n + 1)

        return carry

    lax.fori_loop(0, ITERS, sweep, 0)

    over_group(lambda to: out_copy(to, c).start())
    obuf[c] = ext[ITERS, 1 + k, :, own_rows(s), :]
    over_group(lambda source: out_copy(source, source).wait_recv())

    def back(t, carry):
        at = pl.ds(pl.multiple_of(t * 128, 128), 128)
        for f in range(NF):
            pieces = swap_groups([obuf[t * A + i, f] for i in range(A)], lane8)
            for j in range(A):
                out[f, :, j, at] = pieces[j]
        return carry

    lax.fori_loop(0, CH // A, back, 0)

    def sent(to):
        adj_copy(to, c).wait_send()
        frc_copy(to, c).wait_send()
        out_copy(to, c).wait_send()

    over_group(sent)

    @pl.when(jnp.logical_not(last))
    def _():
        table_copy.wait_send()

    def sweep_sent(n, carry):
        for side in range(2):
            az_copy(n, side).wait_send()

        @pl.when(jnp.logical_not(first))
        def _():
            ax_copy(n, 0).wait_send()

        @pl.when(jnp.logical_not(last))
        def _():
            ax_copy(n, 1).wait_send()

        @pl.when(first)
        def _():
            for to in range(PLANES):
                ex_copy(n, to).wait_send()

        return carry

    lax.fori_loop(0, ITERS, sweep_sent, 0)


def table_tile(owner_device, owner_slot, weight):
    column = (owner_device * A + owner_slot).astype(F32).reshape(A, R).T[:, :, None]
    weights = weight.reshape(A, R).T[:, :, None]
    low = jnp.arange(32)[None, None, :] < 16
    return jnp.where(low, column, weights).reshape(R, A * 32)


def per_device(
    adjoint, forcing, area_scale, azimuth_coupling, axial_coupling,
    inverse, owner_device, owner_slot, weight,
):
    vmem = pl.BlockSpec(memory_space=pltpu.VMEM)
    smem = pl.BlockSpec(memory_space=pltpu.SMEM)
    dma = pltpu.SemaphoreType.DMA
    return pl.pallas_call(
        kernel,
        out_shape=jax.ShapeDtypeStruct(adjoint.shape, F32),
        in_specs=[vmem, vmem, vmem, smem, smem, vmem, vmem],
        out_specs=vmem,
        scratch_shapes=[
            pltpu.VMEM((CH, 2 * NF + 1, R, 128), F32),
            pltpu.VMEM((ITERS + 1, TILES + 2, NF, NR, 128), F32),
            pltpu.VMEM((TILES, NF + 1, NR, 128), F32),
            pltpu.VMEM((ITERS, 2, FOLD, 128), F32),
            pltpu.VMEM((ITERS, 2, FOLD, 128), F32),
            pltpu.VMEM((ITERS, PLANES, FOLD, 128), F32),
            pltpu.VMEM((CH, NF, R, 128), F32),
            pltpu.VMEM((TILES, NR, 128), F32),
            pltpu.VMEM((NR, 128), F32),
            pltpu.VMEM((PLANES, NR, 128), F32),
            pltpu.VMEM((32, NR, 128), F32),
            pltpu.VMEM((2, ROWS, ROWS), BF16),
            pltpu.VMEM((ROWS, TILES * 128), F32),
            pltpu.VMEM((ROWS, 128), F32),
            dma((CH,)), dma((CH,)), dma((CH,)), dma((CH,)), dma((CH,)), dma((CH,)),
            dma((ITERS, 2)), dma((ITERS, 2)), dma((ITERS, 2)), dma((ITERS, 2)),
            dma((ITERS, PLANES)), dma((ITERS, PLANES)),
            dma(()), dma((CH,)), dma((PLANES,)), dma((PLANES,)),
        ],
        compiler_params=pltpu.CompilerParams(
            collective_id=0, has_side_effects=True, vmem_limit_bytes=48 * 1024 * 1024
        ),
    )(
        adjoint, forcing, area_scale, azimuth_coupling, axial_coupling, inverse,
        table_tile(owner_device, owner_slot, weight),
    )


def solution(mesh):
    return jax.shard_map(
        per_device,
        mesh=mesh,
        in_specs=(
            P(None, "span", "passage", None),
            P(None, "span", "passage", None),
            P(None, "span", "passage", None),
            P(),
            P(),
            P("span", None, None),
            P("span", "passage", None, None),
            P("span", "passage", None, None),
            P("span", "passage", None, None),
        ),
        out_specs=P(None, "span", "passage", None),
        check_vma=False,
    )
```

profile of v0, /device:TPU:1, one launch (start us, length us, event | category | flops | bytes accessed | tf_op | source)
XLA Modules:
  0.0 86.4 jit_solution(5969357529478392787)
XLA Ops:
  0.0 0.0 copy-start.7
  0.0 0.0 copy-start.6
  0.0 0.1 broadcast_in_dim.36
  0.1 0.6 copy-done.7
  0.7 0.0 copy-done.6
  0.7 0.0 copy-start.8
  0.7 0.1 copy.10
  0.8 0.6 copy-done.8
  1.4 0.1 copy.11
  1.5 0.1 broadcast_in_dim.40
  1.5 0.1 broadcast_in_dim.41
  1.6 0.1 broadcast_in_dim.38
  1.7 0.1 broadcast_in_dim.39
  1.8 0.0 copy-start.4
  1.8 0.0 copy-start.5
  1.8 0.7 copy-done.4
  2.5 0.0 copy-done.5
  2.5 0.0 copy-start
  2.5 1.1 %copy-done = f32[5,8,4,1024]{3,2,1,0:T(4,128)S(1)} copy-done((f32[5,8,4,1024]{3,2,1,0:T(4,128)S(1)}, f32[5,8,4,1024]{3,2,1,0:T(4,128)}, u32[]{:S(2)}) %copy-start) | copy-done | bytes 655384
  3.6 0.0 copy-start.1
  3.6 1.1 %copy-done.1 = f32[5,8,4,1024]{3,2,1,0:T(4,128)S(1)} copy-done((f32[5,8,4,1024]{3,2,1,0:T(4,128)S(1)}, f32[5,8,4,1024]{3,2,1,0:T(4,128)}, u32[]{:S(2)}) %copy-start.1) | copy-done | bytes 655384
  4.7 0.0 copy-start.2
  4.7 1.0 %copy-done.2 = f32[2,160,160]{2,1,0:T(8,128)S(1)} copy-done((f32[2,160,160]{2,1,0:T(8,128)S(1)}, f32[2,160,160]{2,1,0:T(8,128)}, u32[]{:S(2)}) %copy-start.2) | copy-done | bytes 204824
  5.6 0.0 copy-start.3
  5.6 0.9 %copy-done.3 = f32[1,8,4,1024]{3,2,1,0:T(4,128)S(1)} copy-done((f32[1,8,4,1024]{3,2,1,0:T(4,128)S(1)}, f32[1,8,4,1024]{3,2,1,0:T(4,128)}, u32[]{:S(2)}) %copy-start.3) | copy-done | bytes 131096
  6.5 79.0 %shard_map.91 = f32[5,8,4,1024]{3,2,1,0:T(4,128)S(1)} custom-call(f32[5,8,4,1024]{3,2,1,0:T(4,128)S(1)} %copy-done, f32[5,8,4,1024]{3,2,1,0:T(4,128)S(1)} %copy-done.1, f32[1,8,4,1024]{3,2,1,0:T(4,128)S(1)} %copy-done.3, f32[5,5]{1,0:T(8,128)S(1)} %copy-done.4, f32[5,5]{1,0:T(8,128)S(1)} %copy-done.5, f32[2,160,160]{2,1,0:T(8,128)S(1)} %copy-done.2, ...), custom_call_target="tpu_custom_call" | custom-call | tf_op jit(solution)/shard_map/pallas_call | solution.py:474
  85.5 0.8 copy.13
  (4 shorter events, 0.0 us)
Async XLA Ops:
  0.0 0.7 copy-start.7
  0.0 0.7 copy-start.6
  0.7 0.7 copy-start.8
  1.8 0.7 copy-start.4
  1.8 0.7 copy-start.5
  2.5 1.1 %copy-start = (f32[5,8,4,1024]{3,2,1,0:T(4,128)S(1)}, f32[5,8,4,1024]{3,2,1,0:T(4,128)}, u32[]{:S(2)}) copy-start(f32[5,8,4,1024]{3,2,1,0:T(4,128)} %adj.1) | copy-start | bytes 1966084
  3.6 1.1 %copy-start.1 = (f32[5,8,4,1024]{3,2,1,0:T(4,128)S(1)}, f32[5,8,4,1024]{3,2,1,0:T(4,128)}, u32[]{:S(2)}) copy-start(f32[5,8,4,1024]{3,2,1,0:T(4,128)} %frc.1) | copy-start | bytes 1966084
  4.7 1.0 %copy-start.2 = (f32[2,160,160]{2,1,0:T(8,128)S(1)}, f32[2,160,160]{2,1,0:T(8,128)}, u32[]{:S(2)}) copy-start(f32[2,160,160]{2,1,0:T(8,128)} %inv.1) | copy-start | bytes 614404
  5.6 0.9 %copy-start.3 = (f32[1,8,4,1024]{3,2,1,0:T(4,128)S(1)}, f32[1,8,4,1024]{3,2,1,0:T(4,128)}, u32[]{:S(2)}) copy-start(f32[1,8,4,1024]{3,2,1,0:T(4,128)} %area.1) | copy-start | bytes 393220
where the time goes:
time: 86.7 us; the launch traced here: 86.4 us
  Pallas kernels  79 us (91%)
  local copies, waits for them, and re-layouts  7.33 us (8%)
    pallas_call x1, Pallas kernels, per_device(): pl.pallas_call(kernel, out_shape=jax.ShapeDtypeStruct(adjoint.shape, F32)...  79 us
    unnamed x19, local copies, waits for them, and re-layouts  6.76 us

commit v1 on v0

--- a/solution.py
+++ b/solution.py
@@ -50,8 +50,8 @@
 
 
 def kernel(
-    adj, frc, area, azc, axc, inv, tsend, out,
-    sbuf, ext, fa, psend, hal, inl, obuf, tab, tpl, tall, mtab, lhs, rhs, exitb,
+    adj, frc, area, azc_in, axc_in, inv_in, owner, slot_in, weight_in, out,
+    xin, in_sem, azc, axc, inv, owner_at, slot_at, weight_at, small_sem, tsend, hsend, hrecv, inletb, sbuf, ext, fa, psend, hal, inl, obuf, tab, tpl, tall, mtab, lhs, rhs, exitb,
     a_send, a_recv, f_send, f_recv, o_send, o_recv,
     az_send, az_recv, ax_send, ax_recv, ex_send, ex_recv,
     t_send, t_recv, u_send, u_recv,
@@ -76,6 +76,27 @@
     def own_rows(span):
         return pl.ds(pl.multiple_of(span * R, R), R)
 
+    def load(j, which):
+        src, at, count = ((adj, 0, NF), (frc, NF, NF), (area, 2 * NF, 1))[which]
+        return pltpu.make_async_copy(
+            src.at[:, :, j, :], xin.at[pl.ds(at, count), j], in_sem.at[which, j]
+        )
+
+    small = [
+        pltpu.make_async_copy(source, to, small_sem.at[i])
+        for i, (source, to) in enumerate((
+            (owner, owner_at), (slot_in, slot_at), (weight_in, weight_at),
+            (azc_in, azc), (axc_in, axc), (inv_in.at[k // (TILES // 2)], inv),
+        ))
+    ]
+    for j in range(A):
+        load(j, 0).start()
+    for copy in small:
+        copy.start()
+    for which in range(1, 3):
+        for j in range(A):
+            load(j, which).start()
+
     barrier = pltpu.get_barrier_semaphore()
 
     def greet(plane_at, chunk):
@@ -101,18 +122,31 @@
 
     lane8 = lanes((R, 128))
 
-    def regroup(src, field, slot):
+    def regroup(low, high):
         def body(t, carry):
             at = pl.ds(pl.multiple_of(t * 128, 128), 128)
-            pieces = swap_groups([src[field, :, j, at] for j in range(A)], lane8)
-            for i in range(A):
-                sbuf[t * A + i, slot] = pieces[i]
+            for slot in range(low, high):
+                pieces = swap_groups([xin[slot, j, :, at] for j in range(A)], lane8)
+                for i in range(A):
+                    sbuf[t * A + i, slot] = pieces[i]
             return carry
 
         lax.fori_loop(0, CH // A, body, 0)
 
-    for f in range(NF):
-        regroup(adj, f, f)
+    for copy in small[:3]:
+        copy.wait()
+    diagonal = lax.broadcasted_iota(jnp.int32, (R, R), 0) == lanes((R, R))
+    table = jnp.zeros((R, 128), F32)
+    for j in range(A):
+        column = (owner_at[j] * A + slot_at[j]).astype(F32)
+        for i, row in enumerate((column, weight_at[j])):
+            upright = jnp.sum(jnp.where(diagonal, row, 0.0), axis=1, keepdims=True)
+            table = jnp.where(lane8 // 16 == 2 * j + i, upright, table)
+    tsend[...] = table
+
+    for j in range(A):
+        load(j, 0).wait()
+    regroup(0, NF)
     hal[...] = jnp.zeros_like(hal)
 
     edge = jnp.logical_or(first, last)
@@ -129,7 +163,7 @@
     def adj_copy(to, source):
         return remote(
             sbuf.at[to, pl.ds(0, NF)],
-            ext.at[0, 1 + source % TILES, :, own_rows(source // TILES), :],
+            ext.at[0, source % TILES, :, own_rows(source // TILES), :],
             a_send.at[to], a_recv.at[source], device(plane, to),
         )
 
@@ -142,7 +176,7 @@
 
     def out_copy(to, source):
         return remote(
-            ext.at[ITERS, 1 + to % TILES, :, own_rows(to // TILES), :],
+            ext.at[ITERS, to % TILES, :, own_rows(to // TILES), :],
             obuf.at[source],
             o_send.at[to], o_recv.at[source], device(plane, to),
         )
@@ -164,19 +198,23 @@
     def _():
         table_copy.start()
 
-    for f in range(NF):
-        regroup(frc, f, NF + f)
-    regroup(area, 0, 2 * NF)
+    for which in range(1, 3):
+        for j in range(A):
+            load(j, which).wait()
+    regroup(NF, 2 * NF + 1)
     over_group(lambda to: frc_copy(to, c).start())
 
-    ext[0, 1 + k, :, own_rows(s), :] = sbuf[c, 0:NF]
+    ext[0, k, :, own_rows(s), :] = sbuf[c, 0:NF]
     fa[k, :, own_rows(s), :] = sbuf[c, NF:2 * NF + 1]
 
-    high, low = split(inv[k // (TILES // 2)])
+    for copy in small[3:]:
+        copy.wait()
+    high, low = split(inv[...])
     lhs[0] = high
     lhs[1] = low
 
     xx32 = lanes((NR, 128)) % 32
+    lane32 = lanes((NR, 128))
     lane160 = lanes((ROWS, 128))
     xx160 = lane160 % 32
     lane40 = lanes((FOLD, 128))
@@ -237,9 +275,10 @@
     prv = (c + CH - 1) % CH
 
     def az_copy(n, side):
-        if side == 0:
-            return remote(ext.at[n, 1], ext.at[n, TILES + 1], az_send.at[n, 0], az_recv.at[n, 0], device(down, c))
-        return remote(ext.at[n, TILES], ext.at[n, 0], az_send.at[n, 1], az_recv.at[n, 1], device(up, c))
+        return remote(
+            hsend.at[n, side], hrecv.at[n, side], az_send.at[n, side], az_recv.at[n, side],
+            device(up if side else down, c),
+        )
 
     def ax_copy(n, side):
         if side == 0:
@@ -255,14 +294,23 @@
     def ex_wait(n, source):
         return remote(psend.at[n, 0], inl.at[n, source], ex_send.at[n, source], ex_recv.at[n, source], device(source, 0))
 
+    half80 = lanes((ROWS // 2, 128)) < 64
+
     def send_az(n):
         for side in range(2):
+            tile = ext[n, side * (TILES - 1)].reshape(ROWS, 128)
+            near, far = tile[:ROWS // 2], roll(tile[ROWS // 2:], 64)
+            hsend[n, side] = jnp.where(half80, far, near) if side else jnp.where(half80, near, far)
             az_copy(n, side).start()
+
+    def halo(n, side):
+        packed = hrecv[n, side]
+        return jnp.concatenate([packed, roll(packed, 64)], axis=0)
 
     def send_ax(n):
         edges = [jnp.zeros((FOLD, 128), F32), jnp.zeros((FOLD, 128), F32)]
         for kk in range(TILES):
-            tile = ext[n, 1 + kk].reshape(ROWS, 128)
+            tile = ext[n, kk].reshape(ROWS, 128)
             for g in range(4):
                 rows = tile[g * FOLD:(g + 1) * FOLD]
                 to = 8 * g + kk
@@ -305,9 +353,9 @@
         return total
 
     def azimuth_part(n, kk):
-        here = ext[n, 1 + kk].reshape(ROWS, 128)
-        before = ext[n, kk].reshape(ROWS, 128)
-        after = ext[n, 2 + kk].reshape(ROWS, 128)
+        here = ext[n, kk].reshape(ROWS, 128)
+        before = ext[n, kk - 1].reshape(ROWS, 128) if kk else halo(n, 1)
+        after = ext[n, kk + 1].reshape(ROWS, 128) if kk < TILES - 1 else halo(n, 0)
         plus = roll(jnp.where(lane160 >= 32, here, after), 96)
         minus = roll(jnp.where(lane160 < 96, here, before), 32)
         far = roll(
@@ -320,7 +368,7 @@
             rhs[rows, at] = here[rows] + fa[kk, f] - fa[kk, NF] * couple(az, slope, f)
 
     def axial_part(n, kk, before, after):
-        here = ext[n, 1 + kk].reshape(ROWS, 128)
+        here = ext[n, kk].reshape(ROWS, 128)
         slope = jnp.where(xx160 == 31, roll(after, 31 - kk), roll(here, 127)) - jnp.where(
             xx160 == 0, roll(before, -kk), roll(here, 1)
         )
@@ -341,19 +389,26 @@
             for i in range(PLANES):
                 group = jnp.where(xx40 // 8 == i, roll(inl[n, i], 8 * (i - g)), group)
             groups.append(group)
-        inlet = jnp.concatenate(groups, axis=0)
-        exitb[...] = jnp.zeros_like(exitb)
-        column = lanes((256, 128))
-
-        def one(b, carry):
-            weighted = inlet * jnp.concatenate([mtab[b]] * NF, axis=0)
-            pair = jnp.concatenate(split(weighted), axis=1)
-            place = (b % A) * 32 + b // A
-            ones = (column == place).astype(F32).astype(BF16)
-            exitb[...] += jnp.dot(pair, ones, preferred_element_type=F32)
+        inletb[...] = jnp.concatenate(groups, axis=0)
+
+        def one(f, carry):
+            rows = pl.ds(pl.multiple_of(f * NR, NR), NR)
+            inlet = inletb[rows]
+
+            def summed(b, levels):
+                if not levels:
+                    return inlet * mtab[b]
+                (bit, step), rest = levels[0], levels[1:]
+                zero, one_ = summed(b, rest), summed(b + step, rest)
+                odd = (lane32 // bit) % 2 == 1
+                return jnp.where(odd, one_, zero) + roll(jnp.where(odd, zero, one_), -bit)
+
+            total = summed(0, ((64, 2), (32, 1), (4, 16), (2, 8), (1, 4)))
+            total = total + roll(total, -8)
+            exitb[rows] = total + roll(total, -16)
             return carry
 
-        lax.fori_loop(0, 32, one, 0)
+        lax.fori_loop(0, NF, one, 0)
         arrived = exitb[...]
         for kk in range(TILES):
             at = slice(kk * 128, (kk + 1) * 128)
@@ -365,7 +420,7 @@
         solved = solved + jnp.dot(lhs[1], high, preferred_element_type=F32)
         solved = solved + jnp.dot(lhs[0], high, preferred_element_type=F32)
         for i in range(2):
-            ext[n + 1, 1 + 2 * pair + i] = solved[:, i * 128:(i + 1) * 128].reshape(NF, NR, 128)
+            ext[n + 1, 2 * pair + i] = solved[:, i * 128:(i + 1) * 128].reshape(NF, NR, 128)
 
     def sweep(n, carry):
         for kk in range(1, TILES - 1):
@@ -411,10 +466,17 @@
     lax.fori_loop(0, ITERS, sweep, 0)
 
     over_group(lambda to: out_copy(to, c).start())
-    obuf[c] = ext[ITERS, 1 + k, :, own_rows(s), :]
-    over_group(lambda source: out_copy(source, source).wait_recv())
-
-    def back(t, carry):
+    obuf[c] = ext[ITERS, k, :, own_rows(s), :]
+
+    def back(step, carry):
+        t = (c // A + CH // A - step) % (CH // A)
+        for i in range(A):
+            source = t * A + i
+
+            @pl.when(source != c)
+            def _():
+                out_copy(source, source).wait_recv()
+
         at = pl.ds(pl.multiple_of(t * 128, 128), 128)
         for f in range(NF):
             pieces = swap_groups([obuf[t * A + i, f] for i in range(A)], lane8)
@@ -422,7 +484,7 @@
                 out[f, :, j, at] = pieces[j]
         return carry
 
-    lax.fori_loop(0, CH // A, back, 0)
+    lax.fori_loop(1, CH // A + 1, back, 0)
 
     def sent(to):
         adj_copy(to, c).wait_send()
@@ -455,13 +517,6 @@
         return carry
 
     lax.fori_loop(0, ITERS, sweep_sent, 0)
-
-
-def table_tile(owner_device, owner_slot, weight):
-    column = (owner_device * A + owner_slot).astype(F32).reshape(A, R).T[:, :, None]
-    weights = weight.reshape(A, R).T[:, :, None]
-    low = jnp.arange(32)[None, None, :] < 16
-    return jnp.where(low, column, weights).reshape(R, A * 32)
 
 
 def per_device(
@@ -469,16 +524,29 @@
     inverse, owner_device, owner_slot, weight,
 ):
     vmem = pl.BlockSpec(memory_space=pltpu.VMEM)
-    smem = pl.BlockSpec(memory_space=pltpu.SMEM)
+    hbm = pl.BlockSpec(memory_space=pltpu.HBM)
     dma = pltpu.SemaphoreType.DMA
     return pl.pallas_call(
         kernel,
         out_shape=jax.ShapeDtypeStruct(adjoint.shape, F32),
-        in_specs=[vmem, vmem, vmem, smem, smem, vmem, vmem],
+        in_specs=[hbm] * 9,
         out_specs=vmem,
         scratch_shapes=[
+            pltpu.VMEM((2 * NF + 1, A, R, CH * 32), F32),
+            dma((3, A)),
+            pltpu.SMEM((NF, NF), F32),
+            pltpu.SMEM((NF, NF), F32),
+            pltpu.VMEM((ROWS, ROWS), F32),
+            pltpu.VMEM((A, 1, R), jnp.int32),
+            pltpu.VMEM((A, 1, R), jnp.int32),
+            pltpu.VMEM((A, 1, R), F32),
+            dma((6,)),
+            pltpu.VMEM((R, 128), F32),
+            pltpu.VMEM((ITERS, 2, ROWS // 2, 128), F32),
+            pltpu.VMEM((ITERS, 2, ROWS // 2, 128), F32),
+            pltpu.VMEM((ROWS, 128), F32),
             pltpu.VMEM((CH, 2 * NF + 1, R, 128), F32),
-            pltpu.VMEM((ITERS + 1, TILES + 2, NF, NR, 128), F32),
+            pltpu.VMEM((ITERS + 1, TILES, NF, NR, 128), F32),
             pltpu.VMEM((TILES, NF + 1, NR, 128), F32),
             pltpu.VMEM((ITERS, 2, FOLD, 128), F32),
             pltpu.VMEM((ITERS, 2, FOLD, 128), F32),
@@ -497,11 +565,11 @@
             dma(()), dma((CH,)), dma((PLANES,)), dma((PLANES,)),
         ],
         compiler_params=pltpu.CompilerParams(
-            collective_id=0, has_side_effects=True, vmem_limit_bytes=48 * 1024 * 1024
+            collective_id=0, has_side_effects=True, vmem_limit_bytes=60 * 1024 * 1024
         ),
     )(
         adjoint, forcing, area_scale, azimuth_coupling, axial_coupling, inverse,
-        table_tile(owner_device, owner_slot, weight),
+        owner_device.reshape(A, 1, R), owner_slot.reshape(A, 1, R), weight.reshape(A, 1, R),
     )
 
 

time: 86.7 us -> 69.5 us (0.80)
  Pallas kernels: 79 us -> 67.3 us
  local copies, waits for them, and re-layouts: 7.33 us -> 1.99 us
    pallas_call x1, Pallas kernels: 79 us -> 67.3 us  [per_device(): pl.pallas_call(kernel, out_shape=jax.ShapeDtypeStruct(adjoint.shape, F32)...]
    unnamed x19 -> x1, local copies, waits for them, and re-layouts: 6.76 us -> 1.99 us
where the time goes in v1:
time: 69.5 us; the launch traced here: 69.3 us
  Pallas kernels  67.3 us (97%)
  local copies, waits for them, and re-layouts  1.99 us (3%)
    pallas_call x1, Pallas kernels, per_device(): pl.pallas_call(kernel, out_shape=jax.ShapeDtypeStruct(adjoint.shape, F32)...  67.3 us
    unnamed x1, local copies, waits for them, and re-layouts  1.99 us

profile of v1, /device:TPU:1, one launch (start us, length us, event | category | flops | bytes accessed | tf_op | source)
XLA Modules:
  0.0 69.3 jit_solution(5684023207823971098)
XLA Ops:
  0.0 67.3 %shard_map.91 = f32[5,8,4,1024]{3,2,1,0:T(4,128)} custom-call(f32[5,8,4,1024]{3,2,1,0:T(4,128)} %adj.1, f32[5,8,4,1024]{3,2,1,0:T(4,128)} %frc.1, f32[1,8,4,1024]{3,2,1,0:T(4,128)} %area.1, f32[5,5]{1,0:T(8,128)} %azc_in.1, f32[5,5]{1,0:T(8,128)} %axc_in.1, f32[2,160,160]{2,1,0:T(8,128)} %inv_in.1, s32[4,1,8]{2,1,0:T(1,128)} %bitcast.9, ...), custom_call_target="tpu_custom_call" | custom-call | tf_op jit(solution)/shard_map/pallas_call | solution.py:529
  67.3 2.0 %copy.14 = f32[5,8,4,1024]{3,2,1,0:T(4,128)} copy(f32[5,8,4,1024]{3,2,1,0:T(4,128)} %shard_map.91) | data formatting | bytes 1310720

commit v2 on v1

--- a/solution.py
+++ b/solution.py
@@ -51,7 +51,7 @@
 
 def kernel(
     adj, frc, area, azc_in, axc_in, inv_in, owner, slot_in, weight_in, out,
-    xin, in_sem, azc, axc, inv, owner_at, slot_at, weight_at, small_sem, tsend, hsend, hrecv, inletb, sbuf, ext, fa, psend, hal, inl, obuf, tab, tpl, tall, mtab, lhs, rhs, exitb,
+    xin, in_sem, azc, axc, inv, owner_at, slot_at, weight_at, small_sem, tsend, hsend, hrecv, sbuf, ext, fa, psend, hal, inl, obuf, tab, tpl, tall, mtab, lhs, rhs,
     a_send, a_recv, f_send, f_recv, o_send, o_recv,
     az_send, az_recv, ax_send, ax_recv, ex_send, ex_recv,
     t_send, t_recv, u_send, u_recv,
@@ -77,7 +77,7 @@
         return pl.ds(pl.multiple_of(span * R, R), R)
 
     def load(j, which):
-        src, at, count = ((adj, 0, NF), (frc, NF, NF), (area, 2 * NF, 1))[which]
+        src, at, count = ((adj, 0, NF), (area, NF, 1), (frc, NF + 1, NF))[which]
         return pltpu.make_async_copy(
             src.at[:, :, j, :], xin.at[pl.ds(at, count), j], in_sem.at[which, j]
         )
@@ -144,9 +144,10 @@
             table = jnp.where(lane8 // 16 == 2 * j + i, upright, table)
     tsend[...] = table
 
-    for j in range(A):
-        load(j, 0).wait()
-    regroup(0, NF)
+    for which in range(2):
+        for j in range(A):
+            load(j, which).wait()
+    regroup(0, NF + 1)
     hal[...] = jnp.zeros_like(hal)
 
     edge = jnp.logical_or(first, last)
@@ -162,21 +163,21 @@
 
     def adj_copy(to, source):
         return remote(
-            sbuf.at[to, pl.ds(0, NF)],
+            sbuf.at[to, pl.ds(0, NF + 1)],
             ext.at[0, source % TILES, :, own_rows(source // TILES), :],
             a_send.at[to], a_recv.at[source], device(plane, to),
         )
 
     def frc_copy(to, source):
         return remote(
-            sbuf.at[to, pl.ds(NF, NF + 1)],
+            sbuf.at[to, pl.ds(NF + 1, NF)],
             fa.at[source % TILES, :, own_rows(source // TILES), :],
             f_send.at[to], f_recv.at[source], device(plane, to),
         )
 
     def out_copy(to, source):
         return remote(
-            ext.at[ITERS, to % TILES, :, own_rows(to // TILES), :],
+            ext.at[ITERS, to % TILES, pl.ds(0, NF), own_rows(to // TILES), :],
             obuf.at[source],
             o_send.at[to], o_recv.at[source], device(plane, to),
         )
@@ -198,14 +199,13 @@
     def _():
         table_copy.start()
 
-    for which in range(1, 3):
-        for j in range(A):
-            load(j, which).wait()
-    regroup(NF, 2 * NF + 1)
+    for j in range(A):
+        load(j, 2).wait()
+    regroup(NF + 1, 2 * NF + 1)
     over_group(lambda to: frc_copy(to, c).start())
 
-    ext[0, k, :, own_rows(s), :] = sbuf[c, 0:NF]
-    fa[k, :, own_rows(s), :] = sbuf[c, NF:2 * NF + 1]
+    ext[0, k, :, own_rows(s), :] = sbuf[c, 0:NF + 1]
+    fa[k, :, own_rows(s), :] = sbuf[c, NF + 1:2 * NF + 1]
 
     for copy in small[3:]:
         copy.wait()
@@ -214,7 +214,6 @@
     lhs[1] = low
 
     xx32 = lanes((NR, 128)) % 32
-    lane32 = lanes((NR, 128))
     lane160 = lanes((ROWS, 128))
     xx160 = lane160 % 32
     lane40 = lanes((FOLD, 128))
@@ -259,13 +258,12 @@
             mine = xx32 // 8 == i
             column = jnp.where(mine, roll(tall[i], 8 * i), column)
             weight = jnp.where(mine, roll(tall[i], 8 * i - 16), weight)
-        column = column.astype(jnp.int32) - plane * 32
-
-        def masked(b, carry):
-            mtab[b] = jnp.where(column == b, weight, 0.0)
-            return carry
-
-        lax.fori_loop(0, 32, masked, 0)
+        column = column - (plane * 32).astype(F32)
+        here = (4 * (lanes((NR, 128)) % 8)).astype(F32)
+        for shift in range(8):
+            columns, weights = roll(column, -shift), roll(weight, -shift)
+            for j in range(A):
+                mtab[j, shift] = jnp.where(columns == here + j, weights, 0.0)
         for d in range(1, PLANES):
             plane_table((plane + d) % PLANES).wait_send()
 
@@ -294,11 +292,14 @@
     def ex_wait(n, source):
         return remote(psend.at[n, 0], inl.at[n, source], ex_send.at[n, source], ex_recv.at[n, source], device(source, 0))
 
+    def field(n, kk):
+        return ext[n, kk, 0:NF].reshape(ROWS, 128)
+
     half80 = lanes((ROWS // 2, 128)) < 64
 
     def send_az(n):
         for side in range(2):
-            tile = ext[n, side * (TILES - 1)].reshape(ROWS, 128)
+            tile = field(n, side * (TILES - 1))
             near, far = tile[:ROWS // 2], roll(tile[ROWS // 2:], 64)
             hsend[n, side] = jnp.where(half80, far, near) if side else jnp.where(half80, near, far)
             az_copy(n, side).start()
@@ -310,10 +311,10 @@
     def send_ax(n):
         edges = [jnp.zeros((FOLD, 128), F32), jnp.zeros((FOLD, 128), F32)]
         for kk in range(TILES):
-            tile = ext[n, kk].reshape(ROWS, 128)
-            for g in range(4):
-                rows = tile[g * FOLD:(g + 1) * FOLD]
-                to = 8 * g + kk
+            tile = field(n, kk).reshape(NF, 4, R, 128)
+            for q in range(4):
+                rows = tile[:, q].reshape(FOLD, 128)
+                to = 8 * q + kk
                 edges[0] = jnp.where(xx40 == to, roll(rows, to), edges[0])
                 edges[1] = jnp.where(xx40 == to, roll(rows, to - 31), edges[1])
         psend[n, 0] = edges[0]
@@ -341,8 +342,6 @@
     over_group(wait_adj)
     send_az(0)
     send_ax(0)
-    over_group(wait_frc)
-
     az = [[azc[f, g] * (1.0 / 12.0) for g in range(NF)] for f in range(NF)]
     ax = [[axc[f, g] * 0.5 for g in range(NF)] for f in range(NF)]
 
@@ -352,83 +351,97 @@
             total = total + coefficients[f][g] * slope[g * NR:(g + 1) * NR]
         return total
 
-    def azimuth_part(n, kk):
-        here = ext[n, kk].reshape(ROWS, 128)
-        before = ext[n, kk - 1].reshape(ROWS, 128) if kk else halo(n, 1)
-        after = ext[n, kk + 1].reshape(ROWS, 128) if kk < TILES - 1 else halo(n, 0)
+    def stencils(n, kk):
+        here = field(n, kk)
+        before = field(n, kk - 1) if kk else halo(n, 1)
+        after = field(n, kk + 1) if kk < TILES - 1 else halo(n, 0)
         plus = roll(jnp.where(lane160 >= 32, here, after), 96)
         minus = roll(jnp.where(lane160 < 96, here, before), 32)
         far = roll(
             jnp.where(lane160 >= 64, here, after) - jnp.where(lane160 < 64, here, before), 64
         )
         slope = 8.0 * (plus - minus) - far
-        at = slice(kk * 128, (kk + 1) * 128)
+        along = jnp.where(xx160 == 31, 0.0, roll(here, 127)) - jnp.where(
+            xx160 == 0, 0.0, roll(here, 1)
+        )
         for f in range(NF):
-            rows = slice(f * NR, (f + 1) * NR)
-            rhs[rows, at] = here[rows] + fa[kk, f] - fa[kk, NF] * couple(az, slope, f)
-
-    def axial_part(n, kk, before, after):
-        here = ext[n, kk].reshape(ROWS, 128)
-        slope = jnp.where(xx160 == 31, roll(after, 31 - kk), roll(here, 127)) - jnp.where(
-            xx160 == 0, roll(before, -kk), roll(here, 1)
-        )
-        at = slice(kk * 128, (kk + 1) * 128)
-        for f in range(NF):
-            rows = slice(f * NR, (f + 1) * NR)
-            rhs[rows, at] = rhs[rows, at] - fa[kk, NF] * couple(ax, slope, f)
-
-    def unfold(edge):
-        return jnp.concatenate([roll(edge, -8 * g) for g in range(4)], axis=0)
+            coupled = couple(az, slope, f) + couple(ax, along, f)
+            right = here[f * NR:(f + 1) * NR] - ext[0, kk, NF] * coupled
+            rhs[kk, f] = right.reshape(4, R, 128)
+
+    def couple_edges(n):
+        sides = []
+        for side, sign in ((0, -1.0), (1, 1.0)):
+            edge = hal[n, side].reshape(NF, R, 128)
+            rows = []
+            for f in range(NF):
+                total = ax[f][0] * edge[0]
+                for g in range(1, NF):
+                    total = total + ax[f][g] * edge[g]
+                rows.append(sign * total)
+            sides.append(jnp.concatenate(rows, axis=0))
+        return sides
+
+    def with_edges(kk, edges):
+        right = rhs[kk]
+        groups = []
+        for q in range(4):
+            at = 8 * q + kk
+            edge = jnp.where(
+                xx40 == 31, roll(edges[1], 31 - at), jnp.where(xx40 == 0, roll(edges[0], -at), 0.0)
+            ).reshape(NF, R, 128)
+            scale = ext[0, kk, NF, q * R:(q + 1) * R]
+            groups.append(
+                right[:, q] + fa[kk, :, q * R:(q + 1) * R] - scale[None] * edge
+            )
+        return jnp.stack(groups, axis=1).reshape(ROWS, 128)
 
     def exit_plane(n):
         for source in range(PLANES):
             ex_wait(n, source).wait_recv()
-        groups = []
-        for g in range(4):
-            group = jnp.zeros((FOLD, 128), F32)
+        for q in range(4):
+            inlet = jnp.zeros((FOLD, 128), F32)
             for i in range(PLANES):
-                group = jnp.where(xx40 // 8 == i, roll(inl[n, i], 8 * (i - g)), group)
-            groups.append(group)
-        inletb[...] = jnp.concatenate(groups, axis=0)
-
-        def one(f, carry):
-            rows = pl.ds(pl.multiple_of(f * NR, NR), NR)
-            inlet = inletb[rows]
-
-            def summed(b, levels):
-                if not levels:
-                    return inlet * mtab[b]
-                (bit, step), rest = levels[0], levels[1:]
-                zero, one_ = summed(b, rest), summed(b + step, rest)
-                odd = (lane32 // bit) % 2 == 1
-                return jnp.where(odd, one_, zero) + roll(jnp.where(odd, zero, one_), -bit)
-
-            total = summed(0, ((64, 2), (32, 1), (4, 16), (2, 8), (1, 4)))
+                inlet = jnp.where(xx40 // 8 == i, roll(inl[n, i], 8 * (i - q)), inlet)
+            sums = [None] * A
+            for shift in range(8):
+                moved = roll(inlet, -shift)
+                for j in range(A):
+                    tile = mtab[j, shift, q * R:(q + 1) * R]
+                    term = moved * jnp.concatenate([tile] * NF, axis=0)
+                    sums[j] = term if sums[j] is None else sums[j] + term
+            odd = (lane40 // 32) % 2 == 1
+            pairs = [
+                jnp.where(odd, sums[j + 1], sums[j]) + roll(jnp.where(odd, sums[j], sums[j + 1]), -32)
+                for j in (0, 2)
+            ]
+            upper = lane40 >= 64
+            total = jnp.where(upper, pairs[1], pairs[0]) + roll(
+                jnp.where(upper, pairs[0], pairs[1]), -64
+            )
             total = total + roll(total, -8)
-            exitb[rows] = total + roll(total, -16)
-            return carry
-
-        lax.fori_loop(0, NF, one, 0)
-        arrived = exitb[...]
-        for kk in range(TILES):
-            at = slice(kk * 128, (kk + 1) * 128)
-            rhs[:, at] = rhs[:, at] + jnp.where(xx160 == 31, roll(arrived, 31 - kk), 0.0)
-
-    def solve(n, pair):
-        high, low = split(rhs[:, pair * 256:(pair + 1) * 256])
+            total = total + roll(total, -16)
+            for kk in range(TILES):
+                placed = jnp.where(xx40 == 31, roll(total, 31 - kk), 0.0)
+                rhs[kk, :, q] += placed.reshape(NF, R, 128)
+
+    def solve(n, pair, edges):
+        high, low = split(jnp.concatenate(
+            [with_edges(2 * pair + i, edges) for i in range(2)], axis=1
+        ))
         solved = jnp.dot(lhs[0], low, preferred_element_type=F32)
         solved = solved + jnp.dot(lhs[1], high, preferred_element_type=F32)
         solved = solved + jnp.dot(lhs[0], high, preferred_element_type=F32)
         for i in range(2):
-            ext[n + 1, 2 * pair + i] = solved[:, i * 128:(i + 1) * 128].reshape(NF, NR, 128)
+            ext[n + 1, 2 * pair + i, 0:NF] = solved[:, i * 128:(i + 1) * 128].reshape(NF, NR, 128)
 
     def sweep(n, carry):
         for kk in range(1, TILES - 1):
-            azimuth_part(n, kk)
+            stencils(n, kk)
         for side in range(2):
             az_copy(n, side).wait_recv()
-        azimuth_part(n, 0)
-        azimuth_part(n, TILES - 1)
+        stencils(n, 0)
+        stencils(n, TILES - 1)
 
         @pl.when(jnp.logical_not(first))
         def _():
@@ -438,24 +451,25 @@
         def _():
             ax_wait(n, 1).wait_recv()
 
-        before = unfold(hal[n, 0])
-        after = unfold(hal[n, 1])
-        for kk in range(TILES):
-            axial_part(n, kk, before, after)
+        @pl.when(n == 0)
+        def _():
+            over_group(wait_frc)
+
+        edges = couple_edges(n)
 
         @pl.when(last)
         def _():
             exit_plane(n)
 
-        solve(n, 0)
-        solve(n, 3)
+        solve(n, 0, edges)
+        solve(n, 3, edges)
 
         @pl.when(n < ITERS - 1)
         def _():
             send_az(n + 1)
 
-        solve(n, 1)
-        solve(n, 2)
+        solve(n, 1, edges)
+        solve(n, 2, edges)
 
         @pl.when(n < ITERS - 1)
         def _():
@@ -466,7 +480,7 @@
     lax.fori_loop(0, ITERS, sweep, 0)
 
     over_group(lambda to: out_copy(to, c).start())
-    obuf[c] = ext[ITERS, k, :, own_rows(s), :]
+    obuf[c] = ext[ITERS, k, 0:NF, own_rows(s), :]
 
     def back(step, carry):
         t = (c // A + CH // A - step) % (CH // A)
@@ -544,10 +558,9 @@
             pltpu.VMEM((R, 128), F32),
             pltpu.VMEM((ITERS, 2, ROWS // 2, 128), F32),
             pltpu.VMEM((ITERS, 2, ROWS // 2, 128), F32),
-            pltpu.VMEM((ROWS, 128), F32),
             pltpu.VMEM((CH, 2 * NF + 1, R, 128), F32),
-            pltpu.VMEM((ITERS + 1, TILES, NF, NR, 128), F32),
-            pltpu.VMEM((TILES, NF + 1, NR, 128), F32),
+            pltpu.VMEM((ITERS + 1, TILES, NF + 1, NR, 128), F32),
+            pltpu.VMEM((TILES, NF, NR, 128), F32),
             pltpu.VMEM((ITERS, 2, FOLD, 128), F32),
             pltpu.VMEM((ITERS, 2, FOLD, 128), F32),
             pltpu.VMEM((ITERS, PLANES, FOLD, 128), F32),
@@ -555,10 +568,9 @@
             pltpu.VMEM((TILES, NR, 128), F32),
             pltpu.VMEM((NR, 128), F32),
             pltpu.VMEM((PLANES, NR, 128), F32),
-            pltpu.VMEM((32, NR, 128), F32),
+            pltpu.VMEM((A, 8, NR, 128), F32),
             pltpu.VMEM((2, ROWS, ROWS), BF16),
-            pltpu.VMEM((ROWS, TILES * 128), F32),
-            pltpu.VMEM((ROWS, 128), F32),
+            pltpu.VMEM((TILES, NF, 4, R, 128), F32),
             dma((CH,)), dma((CH,)), dma((CH,)), dma((CH,)), dma((CH,)), dma((CH,)),
             dma((ITERS, 2)), dma((ITERS, 2)), dma((ITERS, 2)), dma((ITERS, 2)),
             dma((ITERS, PLANES)), dma((ITERS, PLANES)),

time: 69.5 us -> 63 us (0.906)
  Pallas kernels: 67.3 us -> 60.8 us
    pallas_call x1, Pallas kernels: 67.3 us -> 60.8 us  [per_device(): pl.pallas_call(kernel, out_shape=jax.ShapeDtypeStruct(adjoint.shape, F32)...]
where the time goes in v2:
time: 63 us; the launch traced here: 62.8 us
  Pallas kernels  60.8 us (97%)
  local copies, waits for them, and re-layouts  1.99 us (3%)
    pallas_call x1, Pallas kernels, per_device(): pl.pallas_call(kernel, out_shape=jax.ShapeDtypeStruct(adjoint.shape, F32)...  60.8 us
    unnamed x1, local copies, waits for them, and re-layouts  1.99 us

profile of v2, /device:TPU:1, one launch (start us, length us, event | category | flops | bytes accessed | tf_op | source)
XLA Modules:
  0.0 62.8 jit_solution(65165924301491933)
XLA Ops:
  0.0 60.8 %shard_map.91 = f32[5,8,4,1024]{3,2,1,0:T(4,128)} custom-call(f32[5,8,4,1024]{3,2,1,0:T(4,128)} %adj.1, f32[5,8,4,1024]{3,2,1,0:T(4,128)} %frc.1, f32[1,8,4,1024]{3,2,1,0:T(4,128)} %area.1, f32[5,5]{1,0:T(8,128)} %azc_in.1, f32[5,5]{1,0:T(8,128)} %axc_in.1, f32[2,160,160]{2,1,0:T(8,128)} %inv_in.1, s32[4,1,8]{2,1,0:T(1,128)} %bitcast.9, ...), custom_call_target="tpu_custom_call" | custom-call | tf_op jit(solution)/shard_map/pallas_call | solution.py:543
  60.8 2.0 %copy.14 = f32[5,8,4,1024]{3,2,1,0:T(4,128)} copy(f32[5,8,4,1024]{3,2,1,0:T(4,128)} %shard_map.91) | data formatting | bytes 1310720

commit v3 on v2

--- a/solution.py
+++ b/solution.py
@@ -20,6 +20,21 @@
 BF16 = jnp.bfloat16
 
 
+def flip(member):
+    span, k = member // TILES, member % TILES
+    at = k + k // 4 * (11 - 2 * k)
+    return span * TILES + at + span % 2 * (7 - 2 * at)
+
+
+def unflip(chunk):
+    span, at = chunk // TILES, chunk % TILES
+    at = at + span % 2 * (7 - 2 * at)
+    return span * TILES + at + at // 4 * (11 - 2 * at)
+
+
+LAST = unflip(CH - 1)
+
+
 def lanes(shape):
     return lax.broadcasted_iota(jnp.int32, shape, len(shape) - 1)
 
@@ -61,8 +76,9 @@
     plane = p // TILES
     k = p % TILES
     c = s * TILES + k
-    first = c == 0
-    last = c == CH - 1
+    chunk = flip(c)
+    first = chunk == 0
+    last = chunk == CH - 1
 
     def device(plane_at, chunk):
         return (plane_at * TILES + chunk % TILES, chunk // TILES)
@@ -86,7 +102,7 @@
         pltpu.make_async_copy(source, to, small_sem.at[i])
         for i, (source, to) in enumerate((
             (owner, owner_at), (slot_in, slot_at), (weight_in, weight_at),
-            (azc_in, azc), (axc_in, axc), (inv_in.at[k // (TILES // 2)], inv),
+            (azc_in, azc), (axc_in, axc), (inv_in.at[chunk % TILES // (TILES // 2)], inv),
         ))
     ]
     for j in range(A):
@@ -113,7 +129,7 @@
     @pl.when(first)
     def _():
         for d in range(1, PLANES):
-            greet((plane + d) % PLANES, CH - 1)
+            greet((plane + d) % PLANES, LAST)
 
     @pl.when(last)
     def _():
@@ -163,14 +179,14 @@
 
     def adj_copy(to, source):
         return remote(
-            sbuf.at[to, pl.ds(0, NF + 1)],
+            sbuf.at[flip(to), pl.ds(0, NF + 1)],
             ext.at[0, source % TILES, :, own_rows(source // TILES), :],
             a_send.at[to], a_recv.at[source], device(plane, to),
         )
 
     def frc_copy(to, source):
         return remote(
-            sbuf.at[to, pl.ds(NF + 1, NF)],
+            sbuf.at[flip(to), pl.ds(NF + 1, NF)],
             fa.at[source % TILES, :, own_rows(source // TILES), :],
             f_send.at[to], f_recv.at[source], device(plane, to),
         )
@@ -178,7 +194,7 @@
     def out_copy(to, source):
         return remote(
             ext.at[ITERS, to % TILES, pl.ds(0, NF), own_rows(to // TILES), :],
-            obuf.at[source],
+            obuf.at[flip(source)],
             o_send.at[to], o_recv.at[source], device(plane, to),
         )
 
@@ -192,7 +208,7 @@
     over_group(lambda to: adj_copy(to, c).start())
 
     table_copy = remote(
-        tsend, tab.at[k, own_rows(s), :], t_send, t_recv.at[c], device(plane, CH - 1)
+        tsend, tab.at[k, own_rows(s), :], t_send, t_recv.at[c], device(plane, LAST)
     )
 
     @pl.when(jnp.logical_not(last))
@@ -204,14 +220,13 @@
     regroup(NF + 1, 2 * NF + 1)
     over_group(lambda to: frc_copy(to, c).start())
 
-    ext[0, k, :, own_rows(s), :] = sbuf[c, 0:NF + 1]
-    fa[k, :, own_rows(s), :] = sbuf[c, NF + 1:2 * NF + 1]
+    ext[0, k, :, own_rows(s), :] = sbuf[chunk, 0:NF + 1]
+    fa[k, :, own_rows(s), :] = sbuf[chunk, NF + 1:2 * NF + 1]
 
     for copy in small[3:]:
         copy.wait()
     high, low = split(inv[...])
-    lhs[0] = high
-    lhs[1] = low
+    lhs[...] = jnp.concatenate([high, low, high], axis=1)
 
     xx32 = lanes((NR, 128)) % 32
     lane160 = lanes((ROWS, 128))
@@ -222,27 +237,23 @@
     def plane_table(plane_to):
         return remote(
             tpl, tall.at[plane], u_send.at[plane_to], u_recv.at[plane],
-            device(plane_to, CH - 1),
+            device(plane_to, LAST),
         )
 
     def plane_table_in(plane_from):
         return remote(
             tpl, tall.at[plane_from], u_send.at[plane_from], u_recv.at[plane_from],
-            device(plane_from, CH - 1),
+            device(plane_from, LAST),
         )
 
     @pl.when(last)
     def _():
         tab[k, own_rows(s), :] = tsend[...]
 
-        def arrived(source, carry):
-            remote(
-                tsend, tab.at[source % TILES, own_rows(source // TILES), :],
-                t_send, t_recv.at[source], device(plane, 0),
-            ).wait_recv()
-            return carry
-
-        lax.fori_loop(0, CH - 1, arrived, 0)
+        over_group(lambda source: remote(
+            tsend, tab.at[source % TILES, own_rows(source // TILES), :],
+            t_send, t_recv.at[source], device(plane, 0),
+        ).wait_recv())
         merged = jnp.zeros((NR, 128), F32)
         for i in range(TILES):
             merged = jnp.where((xx32 == i) | (xx32 == 16 + i), tab[i], merged)
@@ -269,8 +280,8 @@
 
     up = (plane + 1) % PLANES
     down = (plane + PLANES - 1) % PLANES
-    nxt = (c + 1) % CH
-    prv = (c + CH - 1) % CH
+    nxt = unflip((chunk + 1) % CH)
+    prv = unflip((chunk + CH - 1) % CH)
 
     def az_copy(n, side):
         return remote(
@@ -287,7 +298,7 @@
         return remote(psend.at[n, side], hal.at[n, side], ax_send.at[n, side], ax_recv.at[n, side], device(plane, nxt))
 
     def ex_copy(n, to):
-        return remote(psend.at[n, 0], inl.at[n, plane], ex_send.at[n, to], ex_recv.at[n, plane], device(to, CH - 1))
+        return remote(psend.at[n, 0], inl.at[n, plane], ex_send.at[n, to], ex_recv.at[n, plane], device(to, LAST))
 
     def ex_wait(n, source):
         return remote(psend.at[n, 0], inl.at[n, source], ex_send.at[n, source], ex_recv.at[n, source], device(source, 0))
@@ -429,9 +440,7 @@
         high, low = split(jnp.concatenate(
             [with_edges(2 * pair + i, edges) for i in range(2)], axis=1
         ))
-        solved = jnp.dot(lhs[0], low, preferred_element_type=F32)
-        solved = solved + jnp.dot(lhs[1], high, preferred_element_type=F32)
-        solved = solved + jnp.dot(lhs[0], high, preferred_element_type=F32)
+        solved = jnp.dot(lhs[...], jnp.concatenate([high, high, low], axis=0), preferred_element_type=F32)
         for i in range(2):
             ext[n + 1, 2 * pair + i, 0:NF] = solved[:, i * 128:(i + 1) * 128].reshape(NF, NR, 128)
 
@@ -480,12 +489,12 @@
     lax.fori_loop(0, ITERS, sweep, 0)
 
     over_group(lambda to: out_copy(to, c).start())
-    obuf[c] = ext[ITERS, k, 0:NF, own_rows(s), :]
+    obuf[chunk] = ext[ITERS, k, 0:NF, own_rows(s), :]
 
     def back(step, carry):
-        t = (c // A + CH // A - step) % (CH // A)
+        t = (chunk // A + CH // A - step) % (CH // A)
         for i in range(A):
-            source = t * A + i
+            source = unflip(t * A + i)
 
             @pl.when(source != c)
             def _():
@@ -569,7 +578,7 @@
             pltpu.VMEM((NR, 128), F32),
             pltpu.VMEM((PLANES, NR, 128), F32),
             pltpu.VMEM((A, 8, NR, 128), F32),
-            pltpu.VMEM((2, ROWS, ROWS), BF16),
+            pltpu.VMEM((ROWS, 3 * ROWS), BF16),
             pltpu.VMEM((TILES, NF, 4, R, 128), F32),
             dma((CH,)), dma((CH,)), dma((CH,)), dma((CH,)), dma((CH,)), dma((CH,)),
             dma((ITERS, 2)), dma((ITERS, 2)), dma((ITERS, 2)), dma((ITERS, 2)),

time: 63 us -> 61.3 us (0.973)
  Pallas kernels: 60.8 us -> 59.2 us
    pallas_call x1, Pallas kernels: 60.8 us -> 59.2 us  [per_device(): pl.pallas_call(kernel, out_shape=jax.ShapeDtypeStruct(adjoint.shape, F32)...]
where the time goes in v3:
time: 61.3 us; the launch traced here: 61.2 us
  Pallas kernels  59.2 us (97%)
  local copies, waits for them, and re-layouts  1.99 us (3%)
    pallas_call x1, Pallas kernels, per_device(): pl.pallas_call(kernel, out_shape=jax.ShapeDtypeStruct(adjoint.shape, F32)...  59.2 us
    unnamed x1, local copies, waits for them, and re-layouts  1.99 us

profile of v3, /device:TPU:1, one launch (start us, length us, event | category | flops | bytes accessed | tf_op | source)
XLA Modules:
  0.0 61.2 jit_solution(17581006196194107387)
XLA Ops:
  0.0 59.2 %shard_map.91 = f32[5,8,4,1024]{3,2,1,0:T(4,128)} custom-call(f32[5,8,4,1024]{3,2,1,0:T(4,128)} %adj.1, f32[5,8,4,1024]{3,2,1,0:T(4,128)} %frc.1, f32[1,8,4,1024]{3,2,1,0:T(4,128)} %area.1, f32[5,5]{1,0:T(8,128)} %azc_in.1, f32[5,5]{1,0:T(8,128)} %axc_in.1, f32[2,160,160]{2,1,0:T(8,128)} %inv_in.1, s32[4,1,8]{2,1,0:T(1,128)} %bitcast.9, ...), custom_call_target="tpu_custom_call" | custom-call | tf_op jit(solution)/shard_map/pallas_call | solution.py:552
  59.2 2.0 %copy.14 = f32[5,8,4,1024]{3,2,1,0:T(4,128)} copy(f32[5,8,4,1024]{3,2,1,0:T(4,128)} %shard_map.91) | data formatting | bytes 1310720

commit v4 on v3

--- a/solution.py
+++ b/solution.py
@@ -66,7 +66,7 @@
 
 def kernel(
     adj, frc, area, azc_in, axc_in, inv_in, owner, slot_in, weight_in, out,
-    xin, in_sem, azc, axc, inv, owner_at, slot_at, weight_at, small_sem, tsend, hsend, hrecv, sbuf, ext, fa, psend, hal, inl, obuf, tab, tpl, tall, mtab, lhs, rhs,
+    xin, in_sem, azc, axc, inv, owner_at, slot_at, weight_at, small_sem, tsend, hsend, hrecv, sbuf, ext, fa, psend, hal, inl, obuf, tab, tpl, tall, mtab, lhs, rhs, edgeb, areap,
     a_send, a_recv, f_send, f_recv, o_send, o_recv,
     az_send, az_recv, ax_send, ax_recv, ex_send, ex_recv,
     t_send, t_recv, u_send, u_recv,
@@ -152,13 +152,14 @@
     for copy in small[:3]:
         copy.wait()
     diagonal = lax.broadcasted_iota(jnp.int32, (R, R), 0) == lanes((R, R))
-    table = jnp.zeros((R, 128), F32)
+    tables = [jnp.zeros((R, 128), F32)] * 2
     for j in range(A):
         column = (owner_at[j] * A + slot_at[j]).astype(F32)
         for i, row in enumerate((column, weight_at[j])):
             upright = jnp.sum(jnp.where(diagonal, row, 0.0), axis=1, keepdims=True)
-            table = jnp.where(lane8 // 16 == 2 * j + i, upright, table)
-    tsend[...] = table
+            tables[i] = jnp.where(lane8 // 32 == j, upright, tables[i])
+    for i in range(2):
+        tsend[i] = tables[i]
 
     for which in range(2):
         for j in range(A):
@@ -208,7 +209,7 @@
     over_group(lambda to: adj_copy(to, c).start())
 
     table_copy = remote(
-        tsend, tab.at[k, own_rows(s), :], t_send, t_recv.at[c], device(plane, LAST)
+        tsend, tab.at[k, :, own_rows(s), :], t_send, t_recv.at[c], device(plane, LAST)
     )
 
     @pl.when(jnp.logical_not(last))
@@ -248,31 +249,31 @@
 
     @pl.when(last)
     def _():
-        tab[k, own_rows(s), :] = tsend[...]
+        tab[k, :, own_rows(s), :] = tsend[...]
 
         over_group(lambda source: remote(
-            tsend, tab.at[source % TILES, own_rows(source // TILES), :],
+            tsend, tab.at[source % TILES, :, own_rows(source // TILES), :],
             t_send, t_recv.at[source], device(plane, 0),
         ).wait_recv())
-        merged = jnp.zeros((NR, 128), F32)
-        for i in range(TILES):
-            merged = jnp.where((xx32 == i) | (xx32 == 16 + i), tab[i], merged)
-        tpl[...] = merged
+        for which in range(2):
+            merged = tab[0, which]
+            for i in range(1, TILES):
+                merged = jnp.where(xx32 // 4 == i, tab[i, which], merged)
+            tpl[which] = merged
         for d in range(1, PLANES):
             plane_table((plane + d) % PLANES).start()
-        tall[plane] = merged
+        tall[plane] = tpl[...]
         for d in range(1, PLANES):
             plane_table_in((plane + d) % PLANES).wait_recv()
-        column = jnp.zeros((NR, 128), F32)
-        weight = jnp.zeros((NR, 128), F32)
-        for i in range(PLANES):
-            mine = xx32 // 8 == i
-            column = jnp.where(mine, roll(tall[i], 8 * i), column)
-            weight = jnp.where(mine, roll(tall[i], 8 * i - 16), weight)
+        column, weight = tall[0, 0], tall[0, 1]
+        for i in range(1, PLANES):
+            mine = xx32 % 4 == i
+            column = jnp.where(mine, tall[i, 0], column)
+            weight = jnp.where(mine, tall[i, 1], weight)
         column = column - (plane * 32).astype(F32)
-        here = (4 * (lanes((NR, 128)) % 8)).astype(F32)
+        here = (4 * (xx32 // 4)).astype(F32)
         for shift in range(8):
-            columns, weights = roll(column, -shift), roll(weight, -shift)
+            columns, weights = roll(column, -4 * shift), roll(weight, -4 * shift)
             for j in range(A):
                 mtab[j, shift] = jnp.where(columns == here + j, weights, 0.0)
         for d in range(1, PLANES):
@@ -325,9 +326,10 @@
             tile = field(n, kk).reshape(NF, 4, R, 128)
             for q in range(4):
                 rows = tile[:, q].reshape(FOLD, 128)
-                to = 8 * q + kk
-                edges[0] = jnp.where(xx40 == to, roll(rows, to), edges[0])
-                edges[1] = jnp.where(xx40 == to, roll(rows, to - 31), edges[1])
+                to = 4 * kk + q
+                moved = roll(rows, to)
+                edges[0] = jnp.where(xx40 == to, moved, edges[0])
+                edges[1] = jnp.where(xx40 == (to + 31) % 32, moved, edges[1])
         psend[n, 0] = edges[0]
         psend[n, 1] = edges[1]
 
@@ -353,6 +355,16 @@
     over_group(wait_adj)
     send_az(0)
     send_ax(0)
+    scales = [jnp.zeros((R, 128), F32)] * 2
+    for kk in range(TILES):
+        for q in range(4):
+            rows = ext[0, kk, NF, q * R:(q + 1) * R]
+            to = 4 * kk + q
+            scales[0] = jnp.where(lane8 % 32 == (to + 31) % 32, roll(rows, to + 31), scales[0])
+            scales[1] = jnp.where(lane8 % 32 == to, roll(rows, to - 31), scales[1])
+    for side in range(2):
+        areap[side] = scales[side]
+
     az = [[azc[f, g] * (1.0 / 12.0) for g in range(NF)] for f in range(NF)]
     ax = [[axc[f, g] * 0.5 for g in range(NF)] for f in range(NF)]
 
@@ -393,19 +405,27 @@
             sides.append(jnp.concatenate(rows, axis=0))
         return sides
 
-    def with_edges(kk, edges):
-        right = rhs[kk]
-        groups = []
+    def place_edges(n):
+        sides = couple_edges(n)
+        for side in range(2):
+            sides[side] = -jnp.concatenate([areap[side]] * NF, axis=0) * sides[side]
         for q in range(4):
-            at = 8 * q + kk
             edge = jnp.where(
-                xx40 == 31, roll(edges[1], 31 - at), jnp.where(xx40 == 0, roll(edges[0], -at), 0.0)
-            ).reshape(NF, R, 128)
-            scale = ext[0, kk, NF, q * R:(q + 1) * R]
-            groups.append(
-                right[:, q] + fa[kk, :, q * R:(q + 1) * R] - scale[None] * edge
+                xx40 % 4 == 1, roll(sides[0], -30 - q),
+                jnp.where(xx40 % 4 == 0, roll(sides[1], 32 - q), 0.0),
             )
-        return jnp.stack(groups, axis=1).reshape(ROWS, 128)
+            edgeb[:, q] = edge.reshape(NF, R, 128)
+
+    def times_inverse(right):
+        high, low = split(right)
+        return jnp.dot(
+            lhs[...], jnp.concatenate([high, high, low], axis=0), preferred_element_type=F32
+        )
+
+    def add_edges(n, solved, kk):
+        moved = roll(solved, -(4 * kk + 1))
+        edge = jnp.where((xx160 == 0) | (xx160 == 31), moved, 0.0)
+        ext[n + 1, kk, 0:NF] += edge.reshape(NF, NR, 128)
 
     def exit_plane(n):
         for source in range(PLANES):
@@ -413,10 +433,10 @@
         for q in range(4):
             inlet = jnp.zeros((FOLD, 128), F32)
             for i in range(PLANES):
-                inlet = jnp.where(xx40 // 8 == i, roll(inl[n, i], 8 * (i - q)), inlet)
+                inlet = jnp.where(xx40 % 4 == i, roll(inl[n, i], i - q), inlet)
             sums = [None] * A
             for shift in range(8):
-                moved = roll(inlet, -shift)
+                moved = roll(inlet, -4 * shift)
                 for j in range(A):
                     tile = mtab[j, shift, q * R:(q + 1) * R]
                     term = moved * jnp.concatenate([tile] * NF, axis=0)
@@ -430,55 +450,79 @@
             total = jnp.where(upper, pairs[1], pairs[0]) + roll(
                 jnp.where(upper, pairs[0], pairs[1]), -64
             )
-            total = total + roll(total, -8)
-            total = total + roll(total, -16)
-            for kk in range(TILES):
-                placed = jnp.where(xx40 == 31, roll(total, 31 - kk), 0.0)
-                rhs[kk, :, q] += placed.reshape(NF, R, 128)
-
-    def solve(n, pair, edges):
-        high, low = split(jnp.concatenate(
-            [with_edges(2 * pair + i, edges) for i in range(2)], axis=1
+            total = total + roll(total, -1)
+            total = total + roll(total, -2)
+            edgeb[:, q] += jnp.where(xx40 % 4 == 0, roll(total, 32), 0.0).reshape(NF, R, 128)
+
+    def solve(n, pair):
+        tiles = [2 * pair + i for i in range(2)]
+        solved = times_inverse(jnp.concatenate(
+            [rhs[kk].reshape(ROWS, 128) + fa[kk].reshape(ROWS, 128) for kk in tiles], axis=1
         ))
-        solved = jnp.dot(lhs[...], jnp.concatenate([high, high, low], axis=0), preferred_element_type=F32)
         for i in range(2):
             ext[n + 1, 2 * pair + i, 0:NF] = solved[:, i * 128:(i + 1) * 128].reshape(NF, NR, 128)
 
-    def sweep(n, carry):
+    def received_edges(n):
+        @pl.when(jnp.logical_not(first))
+        def _():
+            ax_wait(n, 0).wait_recv()
+
+        @pl.when(jnp.logical_not(last))
+        def _():
+            ax_wait(n, 1).wait_recv()
+
+        place_edges(n)
+
+        @pl.when(last)
+        def _():
+            exit_plane(n)
+
+        return times_inverse(edgeb[...].reshape(ROWS, 128))
+
+    def first_sweep(n):
         for kk in range(1, TILES - 1):
             stencils(n, kk)
         for side in range(2):
             az_copy(n, side).wait_recv()
         stencils(n, 0)
         stencils(n, TILES - 1)
-
-        @pl.when(jnp.logical_not(first))
-        def _():
-            ax_wait(n, 0).wait_recv()
-
-        @pl.when(jnp.logical_not(last))
-        def _():
-            ax_wait(n, 1).wait_recv()
-
-        @pl.when(n == 0)
-        def _():
-            over_group(wait_frc)
-
-        edges = couple_edges(n)
-
-        @pl.when(last)
-        def _():
-            exit_plane(n)
-
-        solve(n, 0, edges)
-        solve(n, 3, edges)
+        solved = received_edges(n)
+        over_group(wait_frc)
+        solve(n, 0)
+        add_edges(n, solved, 0)
+        solve(n, 3)
+        add_edges(n, solved, TILES - 1)
+        send_az(n + 1)
+        add_edges(n, solved, 1)
+        add_edges(n, solved, TILES - 2)
+        for pair in (1, 2):
+            solve(n, pair)
+            add_edges(n, solved, 2 * pair)
+            add_edges(n, solved, 2 * pair + 1)
+        send_ax(n + 1)
+
+    def sweep(n, carry):
+        for kk in range(1, TILES - 1):
+            stencils(n, kk)
+        solve(n, 1)
+        solve(n, 2)
+        for side in range(2):
+            az_copy(n, side).wait_recv()
+        stencils(n, 0)
+        stencils(n, TILES - 1)
+        solve(n, 0)
+        solve(n, 3)
+
+        solved = received_edges(n)
+        add_edges(n, solved, 0)
+        add_edges(n, solved, TILES - 1)
 
         @pl.when(n < ITERS - 1)
         def _():
             send_az(n + 1)
 
-        solve(n, 1, edges)
-        solve(n, 2, edges)
+        for kk in range(1, TILES - 1):
+            add_edges(n, solved, kk)
 
         @pl.when(n < ITERS - 1)
         def _():
@@ -486,7 +530,8 @@
 
         return carry
 
-    lax.fori_loop(0, ITERS, sweep, 0)
+    first_sweep(0)
+    lax.fori_loop(1, ITERS, sweep, 0)
 
     over_group(lambda to: out_copy(to, c).start())
     obuf[chunk] = ext[ITERS, k, 0:NF, own_rows(s), :]
@@ -564,7 +609,7 @@
             pltpu.VMEM((A, 1, R), jnp.int32),
             pltpu.VMEM((A, 1, R), F32),
             dma((6,)),
-            pltpu.VMEM((R, 128), F32),
+            pltpu.VMEM((2, R, 128), F32),
             pltpu.VMEM((ITERS, 2, ROWS // 2, 128), F32),
             pltpu.VMEM((ITERS, 2, ROWS // 2, 128), F32),
             pltpu.VMEM((CH, 2 * NF + 1, R, 128), F32),
@@ -574,12 +619,14 @@
             pltpu.VMEM((ITERS, 2, FOLD, 128), F32),
             pltpu.VMEM((ITERS, PLANES, FOLD, 128), F32),
             pltpu.VMEM((CH, NF, R, 128), F32),
-            pltpu.VMEM((TILES, NR, 128), F32),
-            pltpu.VMEM((NR, 128), F32),
-            pltpu.VMEM((PLANES, NR, 128), F32),
+            pltpu.VMEM((TILES, 2, NR, 128), F32),
+            pltpu.VMEM((2, NR, 128), F32),
+            pltpu.VMEM((PLANES, 2, NR, 128), F32),
             pltpu.VMEM((A, 8, NR, 128), F32),
             pltpu.VMEM((ROWS, 3 * ROWS), BF16),
             pltpu.VMEM((TILES, NF, 4, R, 128), F32),
+            pltpu.VMEM((NF, 4, R, 128), F32),
+            pltpu.VMEM((2, R, 128), F32),
             dma((CH,)), dma((CH,)), dma((CH,)), dma((CH,)), dma((CH,)), dma((CH,)),
             dma((ITERS, 2)), dma((ITERS, 2)), dma((ITERS, 2)), dma((ITERS, 2)),
             dma((ITERS, PLANES)), dma((ITERS, PLANES)),

time: 61.3 us -> 60.5 us (0.987)
  Pallas kernels: 59.2 us -> 58.2 us
    pallas_call x1, Pallas kernels: 59.2 us -> 58.2 us  [per_device(): pl.pallas_call(kernel, out_shape=jax.ShapeDtypeStruct(adjoint.shape, F32)...]
where the time goes in v4:
time: 60.5 us; the launch traced here: 60.2 us
  Pallas kernels  58.2 us (96%)
  local copies, waits for them, and re-layouts  1.99 us (3%)
    pallas_call x1, Pallas kernels, per_device(): pl.pallas_call(kernel, out_shape=jax.ShapeDtypeStruct(adjoint.shape, F32)...  58.2 us
    unnamed x1, local copies, waits for them, and re-layouts  1.99 us

profile of v4, /device:TPU:1, one launch (start us, length us, event | category | flops | bytes accessed | tf_op | source)
XLA Modules:
  0.0 60.2 jit_solution(5826615407811134636)
XLA Ops:
  0.0 58.2 %shard_map.91 = f32[5,8,4,1024]{3,2,1,0:T(4,128)} custom-call(f32[5,8,4,1024]{3,2,1,0:T(4,128)} %adj.1, f32[5,8,4,1024]{3,2,1,0:T(4,128)} %frc.1, f32[1,8,4,1024]{3,2,1,0:T(4,128)} %area.1, f32[5,5]{1,0:T(8,128)} %azc_in.1, f32[5,5]{1,0:T(8,128)} %axc_in.1, f32[2,160,160]{2,1,0:T(8,128)} %inv_in.1, s32[4,1,8]{2,1,0:T(1,128)} %bitcast.9, ...), custom_call_target="tpu_custom_call" | custom-call | tf_op jit(solution)/shard_map/pallas_call | solution.py:597
  58.2 2.0 %copy.14 = f32[5,8,4,1024]{3,2,1,0:T(4,128)} copy(f32[5,8,4,1024]{3,2,1,0:T(4,128)} %shard_map.91) | data formatting | bytes 1310720
